TPU v7x, 32 devices: a whole 2x2x4 slice. The times are simulated.
32 devices in a mesh: tm: 8 (over y, x, core), tile: 4 (over z).
Axes of the slice: x: 2, y: 2, z: 4, core: 2. Of those that a mesh axis runs over, the one named last changes fastest.
Arguments:
- velocity_u: float32 [384, 2, 16, 1024], P('tm', None, None, 'tile'), may hold values from -12 to 12
- velocity_v: float32 [384, 2, 16, 1024], P('tm', None, None, 'tile'), may hold values from -12 to 12
- land_sea: int32 [16, 1024], P(None, 'tile'), may hold values 0 or 1
- bottom_level: int32 [16, 1024], P(None, 'tile'), may hold values from 0 to 2
- spacing_x: float32 [16, 1024], P(None, 'tile'), may hold values from 0.5 to 2
- spacing_y: float32 [16, 1024], P(None, 'tile'), may hold values from 0.5 to 2
Outputs:
- conversion_maps: bfloat16 [384, 2, 16, 1024], P('tm', None, None, 'tile')
- mean_map: float32 [2, 16, 1024], P(None, None, 'tile')
All inputs are finite; a program needn't handle non-finite values. No bound on the sum of `land_sea` on one device may be relied on, other than what follows from the above.
Results may differ from a plain program's by a relative error of at most 0.001.
Values sent between devices are 32-bit elements; how exact they have to be, the bound alone decides.
A program may use at most 64 MiB of HBM per device.

v0:
```python
import jax
import jax.numpy as jnp
from jax import lax
from jax.sharding import PartitionSpec as P

HALF = 24
SNAPS = 48
cutoff_freq = 1.0 / 40.0


def extended(x, sides, width):
    for axis, dim in sides:
        size, length = (lax.axis_size(axis), x.shape[dim])
        up = [(i, (i + 1) % size) for i in range(size - 1)]
        down = [(j, i) for i, j in up]
        last = lax.slice_in_dim(x, length - width, length, axis=dim)
        first = lax.slice_in_dim(x, 0, width, axis=dim)
        before = lax.ppermute(last, axis, up)
        after = lax.ppermute(first, axis, down)
        x = jnp.concatenate([before, x, after], axis=dim)
    return x


def band_matrix(count):
    out_rows = jnp.arange(count, dtype=jnp.int32)[:, None]
    in_cols = jnp.arange(count + 2 * HALF, dtype=jnp.int32)[None, :]
    offset = (in_cols - out_rows - HALF).astype(jnp.float32)
    weights = 2.0 * cutoff_freq * jnp.sinc(2.0 * cutoff_freq * offset) * jnp.sinc(offset / HALF)
    return jnp.where(jnp.abs(offset) <= HALF, weights, jnp.zeros_like(weights))


def lowpass(padded, validity, blocks, block):
    matrix = band_matrix(block)

    def one_block(block_id):
        start = block_id * block
        window = lax.dynamic_slice_in_dim(padded, start, block + 2 * HALF, 0)
        valid_part = lax.dynamic_slice_in_dim(validity, start, block + 2 * HALF, 0)
        weighted = jnp.dot(
            matrix, window, precision=lax.Precision.HIGHEST, preferred_element_type=jnp.float32
        )
        weight_sum = jnp.dot(
            matrix, valid_part, precision=lax.Precision.HIGHEST, preferred_element_type=jnp.float32
        )
        return weighted / weight_sum[:, None]

    result = lax.map(one_block, jnp.arange(blocks, dtype=jnp.int32))
    return result.reshape(blocks * block, padded.shape[1])


def wet_cells(land_sea, bottom_level, levels):
    level_ids = jnp.arange(levels, dtype=jnp.int32)[:, None, None]
    return ((land_sea[None] == 1) & (level_ids < bottom_level[None])).astype(jnp.float32)


def filter_series(series):
    length = series.shape[0]
    flattened = series.reshape(length, -1)
    padded = jnp.pad(flattened, ((HALF, HALF), (0, 0)))
    validity = jnp.pad(jnp.ones((length,), jnp.float32), (HALF, HALF))
    return lowpass(padded, validity, length // SNAPS, SNAPS).reshape(series.shape)


def shards(velocity_u, velocity_v, land_sea, bottom_level, spacing_x, spacing_y):
    block_len = velocity_u.shape[0]
    total_len = block_len * lax.axis_size("tm")
    stacked = jnp.stack([velocity_u, velocity_v], axis=1)
    full_shape = stacked.shape
    flat_cells = stacked.reshape(block_len, 2, -1)
    series_mean = filter_series(
        lax.all_to_all(flat_cells, "tm", split_axis=2, concat_axis=0, tiled=True)
    )
    mean_flat = lax.all_to_all(series_mean, "tm", split_axis=0, concat_axis=2, tiled=True)
    mean_flow = mean_flat.reshape(full_shape)
    eddies = stacked - mean_flow
    wet_mask = wet_cells(land_sea, bottom_level, full_shape[2])
    masked = mean_flow * wet_mask[None, None]
    edge_cols = jnp.concatenate([masked[..., :1], masked[..., -1:]], axis=4)
    edge_ext = extended(edge_cols, (("tile", 4),), 1)
    left_col = edge_ext[..., :1]
    right_col = edge_ext[..., 3:4]
    ahead = jnp.concatenate([masked[..., 1:], right_col], axis=4)
    behind = jnp.concatenate([left_col, masked[..., :-1]], axis=4)
    grad_x = (ahead - behind) * (0.5 / spacing_x)
    row_padded = jnp.pad(masked, ((0, 0), (0, 0), (0, 0), (1, 1), (0, 0)))
    grad_y = (row_padded[..., 2:, :] - row_padded[..., :-2, :]) * (0.5 / spacing_y)
    eddy_u = eddies[:, 0]
    eddy_v = eddies[:, 1]
    total = (
        eddy_u * eddy_u * grad_x[:, 0]
        + eddy_u * eddy_v * (grad_y[:, 0] + grad_x[:, 1])
        + eddy_v * eddy_v * grad_y[:, 1]
    )
    conversion = -wet_mask[None] * total
    summed = lax.psum(jnp.sum(conversion, axis=0), "tm")
    return (conversion.astype(jnp.bfloat16), summed / total_len)


def solution(mesh):
    in_specs = (
        P("tm", None, None, "tile"),
        P("tm", None, None, "tile"),
        P(None, "tile"),
        P(None, "tile"),
        P(None, "tile"),
        P(None, "tile"),
    )
    out_specs = (P("tm", None, None, "tile"), P(None, None, "tile"))
    return jax.shard_map(shards, mesh=mesh, in_specs=in_specs, out_specs=out_specs, check_vma=False)
```

profile of v0, /device:TPU:0, one launch (start us, length us, event | category | flops | bytes accessed | tf_op | source)
XLA Modules:
  0.0 262.7 jit_solution(6098952019784487532)
XLA Ops:
  0.6 0.0 copy-start.3
  0.6 2.7 %stack.18 = f32[48,1,8192]{2,0,1:T(8,128)} reshape(f32[48,2,16,256]{3,2,1,0:T(8,128)} %param.9) | data formatting | bytes 3145728 | tf_op jit(solution)/shard_map/stack | solution.py:67
  3.3 1.4 stack.19
  4.8 2.1 pad_maximum_fusion
  6.9 8.0 %copy.21 = f32[48,2,8192]{0,1,2:T(2,128)} copy(f32[48,2,8192]{2,0,1:T(8,128)S(1)} %pad_maximum_fusion) | data formatting | bytes 6291456 | tf_op jit(solution)/shard_map/stack | solution.py:67
  14.9 16.2 %reshape.50 = f32[8,1,98304]{2,1,0:T(1,128)} reshape(f32[8192,2,48]{2,1,0:T(2,128)} %bitcast.49) | data formatting | bytes 6291456
  31.0 5.4 %all-to-all-start = ((f32[8,1,98304]{2,1,0:T(1,128)}), f32[8,1,98304]{2,1,0:T(1,128)S(1)}, u32[]{:S(2)}, u32[]{:S(2)}) async-start(f32[8,1,98304]{2,1,0:T(1,128)} %reshape.50), calls=%async_computation | async-start | bytes 6291456 | tf_op jit(solution)/shard_map/all_to_all | solution.py:71
  36.5 0.1 pad.13
  36.6 0.7 fusion.42
  37.2 36.8 %all-to-all-done = f32[8,1,98304]{2,1,0:T(1,128)S(1)} async-done(((f32[8,1,98304]{2,1,0:T(1,128)}), f32[8,1,98304]{2,1,0:T(1,128)S(1)}, u32[]{:S(2)}, u32[]{:S(2)}) %all-to-all-start) | async-done | bytes 3145760 | tf_op jit(solution)/shard_map/all_to_all | solution.py:71
  74.1 0.5 broadcast.65
  74.6 11.2 %reduce = f32[8,98304]{1,0:T(8,128)} reduce(f32[8,1,98304]{2,1,0:T(1,128)S(1)} %all-to-all-done, f32[]{:T(128)} %broadcast.65), dimensions={1}, to_apply=%all_to_all.22.reduce_sub_computation | reduce | bytes 6291460 | tf_op jit(solution)/shard_map/all_to_all | solution.py:71
  85.8 19.3 %reshape.51 = f32[8192,2,48]{2,1,0:T(2,128)} reshape(f32[8,98304]{1,0:T(8,128)} %reduce) | data formatting | bytes 6291456
  105.1 7.0 %copy.30 = f32[48,2,8,1024]{3,2,0,1:T(8,128)S(1)} copy(f32[48,2,8,1024]{0,1,3,2:T(2,128)} %bitcast.50) | data formatting | bytes 6291456 | tf_op jit(solution)/shard_map/all_to_all | solution.py:71
  112.1 2.4 copy.23
  114.5 1.4 copy.31
  115.9 0.4 pad.12
  116.3 34.3 %while.11 = (s32[]{:T(128)}, f32[8,48,2048]{2,1,0:T(8,128)}, s32[8]{0:T(128)S(1)}, f32[432,2048]{1,0:T(8,128)S(1)}, f32[48,96]{1,0:T(8,128)}, /*index=5*/f32[432...) while((s32[]{:T(128)}, f32[8,48,2048]{2,1,0:T(8,128)}, s32[8]{0:T(128)S(1)}, ...), condition=%wide.region_1.3_spmd.clone, body=%wide.region_0.2_spmd.clone.sunk | while | flops 113399816 | bytes 1224551 | solution.py:47
  116.4 0.6 dynamic_slice.24
  117.6 0.9 convolution_bitcast_fusion.2
  118.5 2.1 fusion.59
  120.7 0.6 dynamic_slice.24
  121.9 0.9 convolution_bitcast_fusion.2
  122.9 2.1 fusion.59
  125.0 0.6 dynamic_slice.24
  126.2 0.9 convolution_bitcast_fusion.2
  127.1 2.1 fusion.59
  129.2 0.6 dynamic_slice.24
  130.5 0.9 convolution_bitcast_fusion.2
  131.4 2.1 fusion.59
  133.5 0.6 dynamic_slice.24
  134.8 0.9 convolution_bitcast_fusion.2
  135.7 2.1 fusion.59
  137.8 0.6 dynamic_slice.24
  139.0 0.9 convolution_bitcast_fusion.2
  140.0 2.1 fusion.59
  142.1 0.6 dynamic_slice.24
  143.3 0.9 convolution_bitcast_fusion.2
  144.3 2.1 fusion.59
  146.4 0.6 dynamic_slice.24
  147.6 0.9 convolution_bitcast_fusion.2
  148.5 2.1 fusion.59
  150.6 5.6 %reshape_reshape.3 = f32[384,2,1024]{2,1,0:T(2,128)} reshape(f32[8,48,2048]{2,1,0:T(8,128)} %get-tuple-element.38) | data formatting | bytes 6291456 | tf_op jit(solution)/shard_map/reshape;reshape | solution.py:61
  156.2 4.0 %all-to-all-start.1 = ((f32[384,2,1024]{2,1,0:T(2,128)}), f32[384,2,1024]{2,1,0:T(2,128)S(1)}, u32[]{:S(2)}, u32[]{:S(2)}) async-start(f32[384,2,1024]{2,1,0:T(2,128)} %reshape_reshape.3), calls=%async_computation.1 | async-start | bytes 6291456 | tf_op jit(solution)/shard_map/all_to_all | solution.py:73
  160.3 37.7 %all-to-all-done.1 = f32[384,2,1024]{2,1,0:T(2,128)S(1)} async-done(((f32[384,2,1024]{2,1,0:T(2,128)}), f32[384,2,1024]{2,1,0:T(2,128)S(1)}, u32[]{:S(2)}, u32[]{:S(2)}) %all-to-all-start.1) | async-done | bytes 3145760 | tf_op jit(solution)/shard_map/all_to_all | solution.py:73
  198.0 1.0 copy.24
  199.0 1.8 copy.25
  200.8 2.6 reshape.47
  203.4 5.7 %maximum_subtract_fusion = (f32[48,2,2,16,256]{4,3,2,1,0:T(8,128)}, f32[48,2,2,16,256]{4,3,2,1,0:T(8,128)S(1)}) fusion(f32[48,2,2,16,256]{4,3,2,1,0:T(8,128)} %reshape.47, f32[48,1,2,16,256]{4,3,2,1,0:T(8,128)} %bitcast.55, f32[48,1,2,16,256]{4,3,2,1,0:T(8,128)} %bitcast.56, f32[2,16,256]{2,1,0:T(8,128)S(1)} %fusion.15), kind=kLoop, calls=%fused_computation.12 | loop fusion | flops 2359296 | bytes 12615680 | tf_op jit(solution)/shard_map/sub | solution.py:75
  209.1 3.7 %fusion.47 = (f32[48,2,2,16,255]{4,3,2,1,0:T(8,128)}, f32[48,2,2,16,255]{4,3,2,1,0:T(8,128)}) fusion(f32[48,2,2,16,256]{4,3,2,1,0:T(8,128)S(1)} %get-tuple-element.70), kind=kLoop, calls=%fused_computation.85 | loop fusion | bytes 12533760 | tf_op jit(solution)/shard_map/slice | solution.py:83
  212.8 2.3 fusion.46
  215.1 2.2 copy.26
  217.3 1.3 collective-permute-start
  218.6 2.2 copy.28
  220.8 4.7 %collective-permute-start.1 = (f32[48,2,2,16,1]{0,3,4,2,1:T(8,128)S(1)}, f32[48,2,2,16,1]{0,3,4,2,1:T(8,128)S(1)}, u32[]{:S(2)}, u32[]{:S(2)}) collective-permute-start(f32[48,2,2,16,1]{0,3,4,2,1:T(8,128)S(1)} %copy.28), channel_id=1, source_target_pairs={{0,1},{1,2},{2,3},{4,5},{5,6},{6,7},{8,9},{9,10},{10,11},{12,13},{... | collective-permute-start | bytes 36872 | tf_op jit(solution)/shard_map/ppermute | solution.py:18
  225.5 2.4 fusion.7
  228.0 2.4 copy.27
  230.3 0.0 collective-permute-done.1
  230.3 2.4 copy.29
  232.7 4.3 %fusion.8 = f32[48,2,2,16,256]{4,3,2,1,0:T(8,128)S(1)} fusion(f32[48,2,2,16,1]{4,3,2,1,0:T(8,128)} %copy.27, f32[48,2,2,16,255]{4,3,2,1,0:T(8,128)} %get-tuple-element.74, f32[48,2,2,16,255]{4,3,2,1,0:T(8,128)S(1)} %copy-done.2, f32[48,2,2,16,1]{4,3,2,1,0:T(8,128)} %copy.29, f32[16,256]{1,0:T(8,128)S(1)} %broadcast_divide_fusion.1), kind=kLoop, calls=%fused_computation.15 | loop fusion | flops 3145728 | bytes 9453568 | tf_op jit(solution)/shard_map/mul | solution.py:84
  237.0 0.4 copy-done.1
  237.4 2.1 fusion.44
  239.5 22.3 %psum.7 = f32[2,16,256]{2,1,0:T(8,128)S(1)} all-reduce(f32[2,16,256]{2,1,0:T(8,128)S(1)} %get-tuple-element.67), channel_id=1, replica_groups=mesh['tm'=8,'tile'=4] {'tm'}, use_global_device_ids=true, to_apply=%region_3.5 | all-reduce | flops 8192 | bytes 65536 | tf_op jit(solution)/shard_map/psum | solution.py:95
  261.9 0.6 broadcast_multiply_fusion.1
  (23 shorter events, 0.1 us)
Async XLA Ops:
  0.6 2.7 %copy-start.3 = (f32[48,2,16,256]{3,2,1,0:T(8,128)S(1)}, f32[48,2,16,256]{3,2,1,0:T(8,128)}, u32[]{:S(2)}) copy-start(f32[48,2,16,256]{3,2,1,0:T(8,128)} %param.10) | copy-start | bytes 4718596
  31.0 43.1 %all-to-all-start = ((f32[8,1,98304]{2,1,0:T(1,128)}), f32[8,1,98304]{2,1,0:T(1,128)S(1)}, u32[]{:S(2)}, u32[]{:S(2)}) async-start(f32[8,1,98304]{2,1,0:T(1,128)} %reshape.50), calls=%async_computation | async-start | bytes 6291456 | tf_op jit(solution)/shard_map/all_to_all | solution.py:71
  156.2 4.0 %copy-start.5 = (s32[16,256]{1,0:T(8,128)S(1)}, s32[16,256]{1,0:T(8,128)}, u32[]{:S(2)}) copy-start(s32[16,256]{1,0:T(8,128)} %param.11) | copy-start | bytes 49156
  156.2 4.0 %copy-start.6 = (f32[16,256]{1,0:T(8,128)S(1)}, f32[16,256]{1,0:T(8,128)}, u32[]{:S(2)}) copy-start(f32[16,256]{1,0:T(8,128)} %param.13) | copy-start | bytes 49156
  156.2 4.0 %copy-start.7 = (f32[16,256]{1,0:T(8,128)S(1)}, f32[16,256]{1,0:T(8,128)}, u32[]{:S(2)}) copy-start(f32[16,256]{1,0:T(8,128)} %param.14) | copy-start | bytes 49156
  156.2 4.1 %copy-start.4 = (s32[16,256]{1,0:T(8,128)S(1)}, s32[16,256]{1,0:T(8,128)}, u32[]{:S(2)}) copy-start(s32[16,256]{1,0:T(8,128)} %param.12) | copy-start | bytes 49156
  156.2 41.8 %all-to-all-start.1 = ((f32[384,2,1024]{2,1,0:T(2,128)}), f32[384,2,1024]{2,1,0:T(2,128)S(1)}, u32[]{:S(2)}, u32[]{:S(2)}) async-start(f32[384,2,1024]{2,1,0:T(2,128)} %reshape_reshape.3), calls=%async_computation.1 | async-start | bytes 6291456 | tf_op jit(solution)/shard_map/all_to_all | solution.py:73
  217.3 10.7 %collective-permute-start = (f32[48,2,2,16,1]{0,3,4,2,1:T(8,128)S(1)}, f32[48,2,2,16,1]{0,3,4,2,1:T(8,128)S(1)}, u32[]{:S(2)}, u32[]{:S(2)}) collective-permute-start(f32[48,2,2,16,1]{0,3,4,2,1:T(8,128)S(1)} %copy.26), channel_id=1, source_target_pairs={{1,0},{2,1},{3,2},{5,4},{6,5},{7,6},{9,8},{10,9},{11,10},{13,12},{... | collective-permute-start | bytes 36872 | tf_op jit(solution)/shard_map/ppermute | solution.py:19
  220.8 9.6 %collective-permute-start.1 = (f32[48,2,2,16,1]{0,3,4,2,1:T(8,128)S(1)}, f32[48,2,2,16,1]{0,3,4,2,1:T(8,128)S(1)}, u32[]{:S(2)}, u32[]{:S(2)}) collective-permute-start(f32[48,2,2,16,1]{0,3,4,2,1:T(8,128)S(1)} %copy.28), channel_id=1, source_target_pairs={{0,1},{1,2},{2,3},{4,5},{5,6},{6,7},{8,9},{9,10},{10,11},{12,13},{... | collective-permute-start | bytes 36872 | tf_op jit(solution)/shard_map/ppermute | solution.py:18
  228.0 4.7 %copy-start.2 = (f32[48,2,2,16,255]{4,3,2,1,0:T(8,128)S(1)}, f32[48,2,2,16,255]{4,3,2,1,0:T(8,128)}, u32[]{:S(2)}) copy-start(f32[48,2,2,16,255]{4,3,2,1,0:T(8,128)} %get-tuple-element.73) | copy-start | bytes 9400324
  232.7 4.3 %copy-start = (f32[48,2,2,16,256]{4,3,2,1,0:T(8,128)S(1)}, f32[48,2,2,16,256]{4,3,2,1,0:T(8,128)}, u32[]{:S(2)}) copy-start(f32[48,2,2,16,256]{4,3,2,1,0:T(8,128)} %fusion.7) | copy-start | bytes 9437188
  232.7 4.7 %copy-start.1 = (f32[48,2,2,16,256]{4,3,2,1,0:T(8,128)S(1)}, f32[48,2,2,16,256]{4,3,2,1,0:T(8,128)}, u32[]{:S(2)}) copy-start(f32[48,2,2,16,256]{4,3,2,1,0:T(8,128)} %get-tuple-element.69) | copy-start | bytes 9437188
where the time goes:
time: 267 us; the launch traced here: 263 us
  local copies, waits for them, and re-layouts  90.8 us (34%)
  waiting for transfers between devices  74.5 us (28%)
  other arithmetic  29.2 us (11%)
  matrix products  24.2 us (9%)
  blocking collectives  22.3 us (8%)
  starting transfers between devices  15.4 us (6%)
  loops' own time  5.18 us (2%)
    all_to_all x1, waiting for transfers between devices, shards(): lax.all_to_all(series_mean, 'tm', split_axis=0, concat_axis=2, tiled=True)  37.7 us
    unnamed x19, local copies, waits for them, and re-layouts  37.3 us
    all_to_all x1, waiting for transfers between devices, shards(): lax.all_to_all(flat_cells, 'tm', split_axis=2, concat_axis=0, tiled=True)  36.8 us
    psum x1, blocking collectives, shards(): summed = lax.psum(jnp.sum(conversion, axis=0), 'tm')  22.3 us
    dot_general x8, matrix products, one_block(): jnp.dot(matrix, window, precision=lax.Precision.HIGHEST, preferred_elemen...  16.8 us
    another operation x3, local copies, waits for them, and re-layouts, shards(): stacked = jnp.stack([velocity_u, velocity_v], axis=1)  12.1 us
    all_to_all x1, other arithmetic, shards(): lax.all_to_all(flat_cells, 'tm', split_axis=2, concat_axis=0, tiled=True)  11.2 us
    all_to_all x3, local copies, waits for them, and re-layouts, shards(): lax.all_to_all(flat_cells, 'tm', split_axis=2, concat_axis=0, tiled=True)  9.91 us
  transfers between devices with their start and end apart: 4, of which 2 were waited for; matrix products, arithmetic and copies ran while one was open for 3% of the time, Pallas kernels for 0%

commit v1 on v0

--- a/solution.py
+++ b/solution.py
@@ -70,7 +70,15 @@
     series_mean = filter_series(
         lax.all_to_all(flat_cells, "tm", split_axis=2, concat_axis=0, tiled=True)
     )
-    mean_flat = lax.all_to_all(series_mean, "tm", split_axis=0, concat_axis=2, tiled=True)
+    mean_flat = jnp.concatenate(
+        lax.all_to_all(
+            jnp.stack(jnp.split(series_mean, lax.axis_size("tm"), axis=0)),
+            axis_name="tm",
+            split_axis=0,
+            concat_axis=0,
+        ),
+        axis=2,
+    )
     mean_flow = mean_flat.reshape(full_shape)
     eddies = stacked - mean_flow
     wet_mask = wet_cells(land_sea, bottom_level, full_shape[2])

time: 267 us -> 289 us (1.082)
  local copies, waits for them, and re-layouts: 90.8 us -> 113 us
    another operation x1 -> x11, local copies, waits for them, and re-layouts: 5.6 us -> 21.3 us  [the longest x10 16.4 us: shards(): jnp.stack(jnp.split(series_mean, lax.axis_size('tm'), axis=0))]
    unnamed x19 -> x30, local copies, waits for them, and re-layouts: 37.3 us -> 42.4 us
    split x0 -> x1, local copies, waits for them, and re-layouts: none -> 3.24 us  [shards(): jnp.split(series_mean, lax.axis_size('tm'), axis=0)]
where the time goes in v1:
time: 289 us; the launch traced here: 284 us
  local copies, waits for them, and re-layouts  113 us (39%)
  waiting for transfers between devices  74.3 us (26%)
  other arithmetic  29.1 us (10%)
  matrix products  24.2 us (8%)
  blocking collectives  22.3 us (8%)
  starting transfers between devices  15.5 us (5%)
  loops' own time  4.79 us (2%)
    unnamed x30, local copies, waits for them, and re-layouts  42.4 us
    all_to_all x1, waiting for transfers between devices, shards(): lax.all_to_all(jnp.stack(jnp.split(series_mean, lax.axis_size('tm'), axis...  37.7 us
    all_to_all x1, waiting for transfers between devices, shards(): lax.all_to_all(flat_cells, 'tm', split_axis=2, concat_axis=0, tiled=True)  36.6 us
    psum x1, blocking collectives, shards(): summed = lax.psum(jnp.sum(conversion, axis=0), 'tm')  22.3 us
    dot_general x8, matrix products, one_block(): jnp.dot(matrix, window, precision=lax.Precision.HIGHEST, preferred_elemen...  16.7 us
    another operation x10, local copies, waits for them, and re-layouts, shards(): jnp.stack(jnp.split(series_mean, lax.axis_size('tm'), axis=0))  16.4 us
    another operation x3, local copies, waits for them, and re-layouts, shards(): stacked = jnp.stack([velocity_u, velocity_v], axis=1)  12.1 us
    all_to_all x1, other arithmetic, shards(): lax.all_to_all(flat_cells, 'tm', split_axis=2, concat_axis=0, tiled=True)  11.1 us
  transfers between devices with their start and end apart: 4, of which 2 were waited for; matrix products, arithmetic and copies ran while one was open for 3% of the time, Pallas kernels for 0%

profile of v1, /device:TPU:0, one launch (start us, length us, event | category | flops | bytes accessed | tf_op | source)
XLA Modules:
  0.0 284.1 jit_solution(18333886270696611892)
XLA Ops:
  0.6 2.7 stack.45
  3.3 1.4 stack.46
  4.8 2.1 pad_maximum_fusion
  6.9 8.0 %copy.54 = f32[48,2,8192]{0,1,2:T(2,128)} copy(f32[48,2,8192]{2,0,1:T(8,128)S(1)} %pad_maximum_fusion) | data formatting | bytes 6291456 | tf_op jit(solution)/shard_map/stack | solution.py:67
  14.8 16.1 %reshape.65 = f32[8,1,98304]{2,1,0:T(1,128)} reshape(f32[8192,2,48]{2,1,0:T(2,128)} %bitcast.47) | data formatting | bytes 6291456
  31.0 5.7 %all-to-all-start = ((f32[8,1,98304]{2,1,0:T(1,128)}), f32[8,1,98304]{2,1,0:T(1,128)S(1)}, u32[]{:S(2)}, u32[]{:S(2)}) async-start(f32[8,1,98304]{2,1,0:T(1,128)} %reshape.65), calls=%async_computation | async-start | bytes 6291456 | tf_op jit(solution)/shard_map/all_to_all | solution.py:71
  36.8 0.7 fusion.42
  37.4 36.6 %all-to-all-done = f32[8,1,98304]{2,1,0:T(1,128)S(1)} async-done(((f32[8,1,98304]{2,1,0:T(1,128)}), f32[8,1,98304]{2,1,0:T(1,128)S(1)}, u32[]{:S(2)}, u32[]{:S(2)}) %all-to-all-start) | async-done | bytes 3145760 | tf_op jit(solution)/shard_map/all_to_all | solution.py:71
  74.5 11.1 %reduce = f32[8,98304]{1,0:T(8,128)} reduce(f32[8,1,98304]{2,1,0:T(1,128)S(1)} %all-to-all-done, f32[]{:T(128)} %broadcast.65), dimensions={1}, to_apply=%all_to_all.14.reduce_sub_computation | reduce | bytes 6291460 | tf_op jit(solution)/shard_map/all_to_all | solution.py:71
  85.6 19.0 %reshape.66 = f32[8192,2,48]{2,1,0:T(2,128)} reshape(f32[8,98304]{1,0:T(8,128)} %reduce) | data formatting | bytes 6291456
  104.6 7.0 %copy.63 = f32[48,2,8,1024]{3,2,0,1:T(8,128)S(1)} copy(f32[48,2,8,1024]{0,1,3,2:T(2,128)} %bitcast.48) | data formatting | bytes 6291456 | tf_op jit(solution)/shard_map/all_to_all | solution.py:71
  111.6 2.4 copy.56
  114.0 1.4 copy.64
  115.9 33.7 %while.11 = (s32[]{:T(128)}, f32[8,48,2048]{2,1,0:T(8,128)}, s32[8]{0:T(128)S(1)}, f32[432,2048]{1,0:T(8,128)S(1)}, f32[48,96]{1,0:T(8,128)}, /*index=5*/f32[432...) while((s32[]{:T(128)}, f32[8,48,2048]{2,1,0:T(8,128)}, s32[8]{0:T(128)S(1)}, ...), condition=%wide.region_1.3_spmd.clone, body=%wide.region_0.2_spmd.clone.sunk | while | flops 113399816 | bytes 1224551 | solution.py:47
  115.9 0.6 dynamic_slice.24
  117.0 0.9 convolution_bitcast_fusion.2
  118.0 2.1 fusion.60
  121.2 0.9 convolution_bitcast_fusion.2
  122.2 2.1 fusion.60
  125.4 0.9 convolution_bitcast_fusion.2
  126.4 2.1 fusion.60
  129.6 0.9 convolution_bitcast_fusion.2
  130.6 2.1 fusion.60
  133.8 0.9 convolution_bitcast_fusion.2
  134.7 2.1 fusion.60
  138.0 0.9 convolution_bitcast_fusion.2
  138.9 2.1 fusion.60
  142.2 0.9 convolution_bitcast_fusion.2
  143.1 2.1 fusion.60
  146.3 0.9 convolution_bitcast_fusion.2
  147.3 2.1 fusion.60
  149.5 3.2 %fusion.48 = (f32[1,48,2048]{2,1,0:T(8,128)}, f32[1,48,2048]{2,1,0:T(8,128)}, f32[1,48,2048]{2,1,0:T(8,128)S(1)}, f32[1,48,2048]{2,1,0:T(8,128)}, f32[1,48,2048]...) fusion(f32[8,48,2048]{2,1,0:T(8,128)} %get-tuple-element.38), kind=kLoop, calls=%fused_computation.94 | loop fusion | bytes 6291456 | tf_op jit(solution)/shard_map/split | solution.py:75
  152.8 1.1 stack.48
  153.9 1.0 constant_dynamic-update-slice_fusion.7
  154.9 2.1 stack.49
  157.0 2.1 stack.50
  159.0 2.1 stack.51
  161.1 2.1 stack.52
  163.2 1.1 stack.53
  164.2 1.3 stack.54
  165.6 2.1 stack.55
  167.6 1.1 constant_dynamic-update-slice_fusion.6
  168.8 1.0 constant_dynamic-update-slice_fusion.5
  169.8 1.0 constant_dynamic-update-slice_fusion.4
  170.9 1.0 constant_dynamic-update-slice_fusion.3
  172.1 2.6 copy.57
  174.7 3.8 %all-to-all-start.1 = ((f32[8,48,2,1024]{3,1,2,0:T(8,128)}), f32[8,48,2,1024]{3,1,2,0:T(8,128)S(1)}, u32[]{:S(2)}, u32[]{:S(2)}) async-start(f32[8,48,2,1024]{3,1,2,0:T(8,128)} %copy.57), calls=%async_computation.1 | async-start | bytes 6291456 | tf_op jit(solution)/shard_map/all_to_all | solution.py:74
  178.6 37.7 %all-to-all-done.1 = f32[8,48,2,1024]{3,1,2,0:T(8,128)S(1)} async-done(((f32[8,48,2,1024]{3,1,2,0:T(8,128)}), f32[8,48,2,1024]{3,1,2,0:T(8,128)S(1)}, u32[]{:S(2)}, u32[]{:S(2)}) %all-to-all-start.1) | async-done | bytes 3145760 | tf_op jit(solution)/shard_map/all_to_all | solution.py:74
  216.3 3.5 %copy.58 = f32[48,2,8,1024]{3,2,1,0:T(8,128)} copy(f32[48,2,8,1024]{3,0,1,2:T(8,128)S(1)} %bitcast.49) | data formatting | bytes 6291456 | tf_op jit(solution)/shard_map/reshape | solution.py:73
  219.8 4.8 %reshape_reshape.4 = f32[48,2,2,16,256]{4,3,2,1,0:T(8,128)} reshape(f32[48,2,8,1024]{3,2,1,0:T(8,128)} %copy.58) | data formatting | bytes 6291456 | tf_op jit(solution)/shard_map/reshape;reshape | solution.py:82
  224.6 5.7 %maximum_subtract_fusion = (f32[48,2,2,16,256]{4,3,2,1,0:T(8,128)}, f32[48,2,2,16,256]{4,3,2,1,0:T(8,128)S(1)}) fusion(f32[48,2,2,16,256]{4,3,2,1,0:T(8,128)} %reshape_reshape.4, f32[48,1,2,16,256]{4,3,2,1,0:T(8,128)} %bitcast.53, f32[48,1,2,16,256]{4,3,2,1,0:T(8,128)} %bitcast.54, f32[2,16,256]{2,1,0:T(8,128)S(1)} %fusion.15), kind=kLoop, calls=%fused_computation.12 | loop fusion | flops 2359296 | bytes 12615680 | tf_op jit(solution)/shard_map/sub | solution.py:83
  230.3 3.7 %fusion.47 = (f32[48,2,2,16,255]{4,3,2,1,0:T(8,128)}, f32[48,2,2,16,255]{4,3,2,1,0:T(8,128)}) fusion(f32[48,2,2,16,256]{4,3,2,1,0:T(8,128)S(1)} %get-tuple-element.72), kind=kLoop, calls=%fused_computation.93 | loop fusion | bytes 12533760 | tf_op jit(solution)/shard_map/slice | solution.py:91
  234.0 2.3 fusion.46
  236.3 2.2 copy.59
  238.5 1.3 collective-permute-start
  239.8 2.2 copy.61
  242.0 4.8 %collective-permute-start.1 = (f32[48,2,2,16,1]{0,3,4,2,1:T(8,128)S(1)}, f32[48,2,2,16,1]{0,3,4,2,1:T(8,128)S(1)}, u32[]{:S(2)}, u32[]{:S(2)}) collective-permute-start(f32[48,2,2,16,1]{0,3,4,2,1:T(8,128)S(1)} %copy.61), channel_id=1, source_target_pairs={{0,1},{1,2},{2,3},{4,5},{5,6},{6,7},{8,9},{9,10},{10,11},{12,13},{... | collective-permute-start | bytes 36872 | tf_op jit(solution)/shard_map/ppermute | solution.py:18
  246.8 2.4 fusion.7
  249.2 2.4 copy.60
  251.6 2.4 copy.62
  254.0 4.3 %fusion.8 = f32[48,2,2,16,256]{4,3,2,1,0:T(8,128)S(1)} fusion(f32[48,2,2,16,1]{4,3,2,1,0:T(8,128)} %copy.60, f32[48,2,2,16,255]{4,3,2,1,0:T(8,128)} %get-tuple-element.76, f32[48,2,2,16,255]{4,3,2,1,0:T(8,128)S(1)} %copy-done.2, f32[48,2,2,16,1]{4,3,2,1,0:T(8,128)} %copy.62, f32[16,256]{1,0:T(8,128)S(1)} %broadcast_divide_fusion.1), kind=kLoop, calls=%fused_computation.15 | loop fusion | flops 3145728 | bytes 9453568 | tf_op jit(solution)/shard_map/mul | solution.py:92
  258.7 2.1 fusion.44
  260.8 22.3 %psum.7 = f32[2,16,256]{2,1,0:T(8,128)S(1)} all-reduce(f32[2,16,256]{2,1,0:T(8,128)S(1)} %get-tuple-element.69), channel_id=1, replica_groups=mesh['tm'=8,'tile'=4] {'tm'}, use_global_device_ids=true, to_apply=%region_3.5 | all-reduce | flops 8192 | bytes 65536 | tf_op jit(solution)/shard_map/psum | solution.py:103
  283.2 0.6 broadcast_multiply_fusion.1
  (43 shorter events, 5.7 us)
Async XLA Ops:
  0.6 2.7 copy-start.3
  31.0 43.1 %all-to-all-start = ((f32[8,1,98304]{2,1,0:T(1,128)}), f32[8,1,98304]{2,1,0:T(1,128)S(1)}, u32[]{:S(2)}, u32[]{:S(2)}) async-start(f32[8,1,98304]{2,1,0:T(1,128)} %reshape.65), calls=%async_computation | async-start | bytes 6291456 | tf_op jit(solution)/shard_map/all_to_all | solution.py:71
  167.6 4.3 %copy-start.5 = (f32[1,48,2,1024]{3,2,1,0:T(2,128)S(1)}, f32[1,48,2,1024]{3,2,1,0:T(2,128)}, u32[]{:S(2)}) copy-start(f32[1,48,2,1024]{3,2,1,0:T(2,128)} %stack.53) | copy-start | bytes 1179652
  167.6 4.4 %copy-start.4 = (f32[1,48,2,1024]{3,2,1,0:T(2,128)S(1)}, f32[1,48,2,1024]{3,2,1,0:T(2,128)}, u32[]{:S(2)}) copy-start(f32[1,48,2,1024]{3,2,1,0:T(2,128)} %stack.55) | copy-start | bytes 1179652
  174.7 3.8 %copy-start.7 = (s32[16,256]{1,0:T(8,128)S(1)}, s32[16,256]{1,0:T(8,128)}, u32[]{:S(2)}) copy-start(s32[16,256]{1,0:T(8,128)} %param.11) | copy-start | bytes 49156
  174.7 3.8 %copy-start.8 = (f32[16,256]{1,0:T(8,128)S(1)}, f32[16,256]{1,0:T(8,128)}, u32[]{:S(2)}) copy-start(f32[16,256]{1,0:T(8,128)} %param.13) | copy-start | bytes 49156
  174.7 3.9 %copy-start.9 = (f32[16,256]{1,0:T(8,128)S(1)}, f32[16,256]{1,0:T(8,128)}, u32[]{:S(2)}) copy-start(f32[16,256]{1,0:T(8,128)} %param.14) | copy-start | bytes 49156
  174.7 3.9 %copy-start.6 = (s32[16,256]{1,0:T(8,128)S(1)}, s32[16,256]{1,0:T(8,128)}, u32[]{:S(2)}) copy-start(s32[16,256]{1,0:T(8,128)} %param.12) | copy-start | bytes 49156
  174.7 41.6 %all-to-all-start.1 = ((f32[8,48,2,1024]{3,1,2,0:T(8,128)}), f32[8,48,2,1024]{3,1,2,0:T(8,128)S(1)}, u32[]{:S(2)}, u32[]{:S(2)}) async-start(f32[8,48,2,1024]{3,1,2,0:T(8,128)} %copy.57), calls=%async_computation.1 | async-start | bytes 6291456 | tf_op jit(solution)/shard_map/all_to_all | solution.py:74
  238.5 10.7 %collective-permute-start = (f32[48,2,2,16,1]{0,3,4,2,1:T(8,128)S(1)}, f32[48,2,2,16,1]{0,3,4,2,1:T(8,128)S(1)}, u32[]{:S(2)}, u32[]{:S(2)}) collective-permute-start(f32[48,2,2,16,1]{0,3,4,2,1:T(8,128)S(1)} %copy.59), channel_id=1, source_target_pairs={{1,0},{2,1},{3,2},{5,4},{6,5},{7,6},{9,8},{10,9},{11,10},{13,12},{... | collective-permute-start | bytes 36872 | tf_op jit(solution)/shard_map/ppermute | solution.py:19
  242.0 9.6 %collective-permute-start.1 = (f32[48,2,2,16,1]{0,3,4,2,1:T(8,128)S(1)}, f32[48,2,2,16,1]{0,3,4,2,1:T(8,128)S(1)}, u32[]{:S(2)}, u32[]{:S(2)}) collective-permute-start(f32[48,2,2,16,1]{0,3,4,2,1:T(8,128)S(1)} %copy.61), channel_id=1, source_target_pairs={{0,1},{1,2},{2,3},{4,5},{5,6},{6,7},{8,9},{9,10},{10,11},{12,13},{... | collective-permute-start | bytes 36872 | tf_op jit(solution)/shard_map/ppermute | solution.py:18
  249.2 4.7 %copy-start.2 = (f32[48,2,2,16,255]{4,3,2,1,0:T(8,128)S(1)}, f32[48,2,2,16,255]{4,3,2,1,0:T(8,128)}, u32[]{:S(2)}) copy-start(f32[48,2,2,16,255]{4,3,2,1,0:T(8,128)} %get-tuple-element.75) | copy-start | bytes 9400324
  254.0 4.3 %copy-start = (f32[48,2,2,16,256]{4,3,2,1,0:T(8,128)S(1)}, f32[48,2,2,16,256]{4,3,2,1,0:T(8,128)}, u32[]{:S(2)}) copy-start(f32[48,2,2,16,256]{4,3,2,1,0:T(8,128)} %fusion.7) | copy-start | bytes 9437188
  254.0 4.7 %copy-start.1 = (f32[48,2,2,16,256]{4,3,2,1,0:T(8,128)S(1)}, f32[48,2,2,16,256]{4,3,2,1,0:T(8,128)}, u32[]{:S(2)}) copy-start(f32[48,2,2,16,256]{4,3,2,1,0:T(8,128)} %get-tuple-element.71) | copy-start | bytes 9437188
